TPU v7x, 256 devices: a whole 4x4x8 slice. The times are simulated.
256 devices in a mesh: dp: 8 (over z), graph: 32 (over x, y, core).
Axes of the slice: x: 4, y: 4, z: 8, core: 2. Of those that a mesh axis runs over, the one named last changes fastest.
Arguments:
- node_feats: bfloat16 [8, 224, 49, 256], P('dp', 'graph'), may hold values from -0.125 to 0.125
- node_grads: bfloat16 [8, 224, 49, 256], P('dp', 'graph'), may hold values from -1.75 to 1.75
- node_row: int32 [8, 224], P('dp'), may hold values from 0 to 223, as said below
- edge_src: int32 [8, 16384], P('dp', 'graph'), may hold values from 0 to 223, as said below
- edge_tgt: int32 [8, 16384], P('dp', 'graph'), may hold values from 0 to 223, as said below
- edge_rot: int32 [8, 16384], P('dp', 'graph'), may hold values from 0 to 2047
- edge_len: float32 [8, 16384], P('dp', 'graph'), may hold values from 0.5 to 11.5
- edge_count: int32 [8, 32], P('dp', 'graph'), may hold values from 64 to 512, as said below
- rotations: bfloat16 [2048, 7, 49], replicated, as said below
- w_zero: bfloat16 [1792, 1792], replicated, may hold values from -0.125 to 0.125
- w_radial: float32 [600, 256], replicated, may hold values from -3 to 3
Outputs:
- node_grad: float32 [8, 224, 49, 256], P('dp', 'graph')
- weight_grad: float32 [1792, 1792], P('graph')
Inputs may be any that keep to these rules, and one draw needn't show every extreme that they name: Each row of node_row is a permutation: atom i of a batch graph is held at row node_row[b, i], and graph index g holds rows g * 7 to (g + 1) * 7 - 1. `edge_tgt`: for every slot of the block of graph index g, the target atom is held at one of the rows g * 7 to (g + 1) * 7 - 1. `edge_src`: among the 512 slots of the block of one index of graph, at most 24 have source atoms held by the same index of graph; in every batch graph one index of graph holds the source atoms of exactly 24 live slots of every block. The first edge_count[b, g] slots of a block are live, the others are padding with valid ids; in every batch graph one index of graph has all 512 slots live. `rotations`: row l of each rotation is zero outside the coefficients of degree l (coefficients l * l to l * l + 2 l).
All inputs are finite; a program needn't handle non-finite values.
Results may differ from a plain program's by a relative error of at most 0.0041.
Values may be sent and summed in bfloat16 or wider, within the bound.
A program may use at most 256 MiB of HBM per device.

v0:
```python
import jax
import jax.numpy as jnp
from jax import lax
from jax.sharding import PartitionSpec as P

BLOCK = 256
CUTOFF = 12.0


def radial_profile(lengths, w_radial):
    gauss_count = w_radial.shape[0]
    spacing = CUTOFF / (gauss_count - 1)
    centers = jnp.arange(gauss_count).astype(jnp.float32) * spacing
    basis = jnp.exp(-0.5 / (2.0 * spacing) ** 2 * (lengths[:, None] - centers[None, :]) ** 2)
    return jnp.dot(
        basis, w_radial, precision=lax.Precision.HIGHEST, preferred_element_type=jnp.float32
    )


def find_rows(atom_ids, row_table):
    matches = atom_ids[:, None] == jnp.arange(row_table.shape[0], dtype=jnp.int32)[None, :]
    return jnp.sum(jnp.where(matches, row_table[None, :], 0), axis=1)


def forward_rows(turning, source, radial):
    rotated = jnp.einsum("bij,bjc->bic", turning, source, preferred_element_type=jnp.float32)
    return (rotated * radial[:, None, :]).astype(jnp.bfloat16)


def backward_terms(edge_in, target, turning, radial, w_zero):
    edge_grad = jnp.einsum(
        "bij,bjc->bic", turning, target, preferred_element_type=jnp.float32
    ).astype(jnp.bfloat16)
    edge_rows = edge_in.shape[0]
    flat_in = edge_in.reshape(edge_rows, -1)
    flat_grad = edge_grad.reshape(edge_rows, -1)
    weight_term = lax.dot_general(
        flat_in, flat_grad, (((0,), (0,)), ((), ())), preferred_element_type=jnp.float32
    )
    hidden = lax.dot_general(
        flat_grad, w_zero, (((1,), (1,)), ((), ())), preferred_element_type=jnp.float32
    )
    returned = (hidden.reshape(edge_in.shape) * radial[:, None, :]).astype(jnp.bfloat16)
    return (weight_term, returned)


def spread_back(turning, returned):
    return jnp.einsum("bij,bic->bjc", turning, returned, preferred_element_type=jnp.float32)


def per_device(
    node_feats,
    node_grads,
    node_row,
    edge_src,
    edge_tgt,
    edge_rot,
    edge_len,
    edge_count,
    rotations,
    w_zero,
    w_radial,
):
    node_dev = node_feats.shape[1]
    own_index = lax.axis_index("graph")
    row_table = node_row[0]
    grad_table = node_grads[0]
    source_ids = edge_src[0]
    target_rows = find_rows(edge_tgt[0], row_table) - own_index * node_dev
    turn_ids = edge_rot[0]
    lengths = edge_len[0]
    live_count = edge_count[0, 0]
    source_rows = find_rows(source_ids, row_table)
    square = w_zero.shape[0]
    blocks = (live_count + BLOCK - 1) // BLOCK
    sources_all = lax.all_gather(node_feats, "graph", axis=1, tiled=True)[0]

    def advance(step_index, carry):
        weight_acc, node_acc = carry
        first = step_index * BLOCK
        here_source = lax.dynamic_slice_in_dim(source_rows, first, BLOCK)
        here_target = lax.dynamic_slice_in_dim(target_rows, first, BLOCK)
        here_turn = lax.dynamic_slice_in_dim(turn_ids, first, BLOCK)
        here_length = lax.dynamic_slice_in_dim(lengths, first, BLOCK)
        alive_mask = (first + jnp.arange(BLOCK, dtype=jnp.int32) < live_count).astype(jnp.float32)
        radial = radial_profile(here_length, w_radial) * alive_mask[:, None]
        turning = rotations[here_turn]
        edge_in = forward_rows(turning, sources_all[here_source], radial)
        weight_term, returned = backward_terms(
            edge_in, grad_table[here_target], turning, radial, w_zero
        )
        return (
            weight_acc + weight_term,
            node_acc.at[here_source].add(spread_back(turning, returned)),
        )

    start_state = (
        jnp.zeros((square, square), jnp.float32),
        jnp.zeros(sources_all.shape, jnp.float32),
    )
    weight_acc, node_acc = lax.fori_loop(0, blocks, advance, start_state)
    node_part = lax.psum_scatter(node_acc[None], "graph", scatter_dimension=1, tiled=True)
    rows_part = lax.psum_scatter(weight_acc, "graph", scatter_dimension=0, tiled=True)
    weight_grad = lax.psum(rows_part, "dp")
    return (node_part, weight_grad)


def solution(mesh):
    placed = (
        P("dp", "graph", None, None),
        P("dp", "graph", None, None),
        P("dp", None),
        P("dp", "graph"),
        P("dp", "graph"),
        P("dp", "graph"),
        P("dp", "graph"),
        P("dp", "graph"),
        P(),
        P(),
        P(),
    )
    return jax.shard_map(
        per_device,
        mesh=mesh,
        in_specs=placed,
        out_specs=(P("dp", "graph", None, None), P("graph", None)),
        check_vma=False,
    )
```

profile of v0, /device:TPU:2, one launch (start us, length us, event | category | flops | bytes accessed | tf_op | source)
XLA Modules:
  0.0 616.0 jit_solution(6712216942642518904)
XLA Ops:
  7.2 0.0 all-gather.2.cloned.1.call-start
  7.2 0.7 all-gather.2.cloned.1.call-update
  7.9 0.0 reduce-scatter.2.cloned.1.call-start
  8.6 5.6 copy.34
  14.2 0.9 select_reduce_fusion
  15.1 52.0 %all-gather.2.cloned.1.call-done = bf16[1,224,49,256]{3,2,0,1:T(8,128)(2,1)} async-done(((bf16[1,7,49,256]{3,2,0,1:T(8,128)(2,1)}), bf16[1,224,49,256]{3,2,0,1:T(8,128)(2,1)}) %all-gather.2.cloned.1.call-update) | async-done | bytes 5619728 | tf_op jit(solution)/shard_map/all_gather | solution.py:76
  67.1 5.5 broadcast_in_dim.44
  72.6 0.0 copy-start
  72.6 0.0 copy-start.2
  72.6 0.0 copy-start.3
  72.6 0.0 copy-start.4
  72.6 5.4 broadcast_in_dim.45
  78.0 0.0 copy-done
  78.1 0.0 copy-done.2
  78.1 0.0 copy-done.3
  78.1 0.0 copy-done.4
  78.1 100.3 %while.12 = (s32[]{:T(128)}, f32[1792,1792]{1,0:T(8,128)}, f32[224,49,256]{2,1,0:T(8,128)}, s32[]{:T(128)}, s32[512]{0:T(512)S(1)}, /*index=5*/bf16[2048,7,49]{2...) while((s32[]{:T(128)}, f32[1792,1792]{1,0:T(8,128)}, ...), condition=%wide.region_4.5_spmd, body=%wide.region_2.4_spmd.sunk | while | flops 3904316672 | bytes 142397968 | solution.py:101
  78.3 0.1 compare_select_fusion.5
  78.4 3.0 gather_fusion
  81.4 0.1 compare_select_fusion.6
  81.5 6.8 %gather_fusion.1 = bf16[256,49,256]{2,1,0:T(8,128)(2,1)} fusion(bf16[224,49,256]{2,1,0:T(8,128)(2,1)} %get-tuple-element.287, s32[1024]{0:T(1024)S(1)} %pad_clamp_fusion.7), kind=kCustom, calls=%fused_computation.1.clone.1 | custom fusion | bytes 12846080 | tf_op jit(solution)/shard_map/while/body/gather | solution.py:88
  88.3 0.1 dynamic_slice.20
  88.4 0.6 compare_convert_fusion.2
  89.0 0.9 convolution_multiply_fusion.2
  89.9 4.4 multiply_convert_fusion.2
  94.4 0.8 copy.49
  95.2 4.0 gather_fusion.2
  99.2 4.4 convolution_convert_fusion.2
  103.6 1.6 copy.50
  105.1 11.9 %convolution_add_fusion.2 = f32[1792,1792]{1,0:T(8,128)} fusion(f32[1792,1792]{1,0:T(8,128)} %get-tuple-element.263, bf16[256,1792]{0,1:T(8,128)(2,1)S(1)} %bitcast.58, bf16[256,1792]{0,1:T(8,128)(2,1)} %bitcast.59), kind=kOutput, calls=%fused_computation.4.clone.1 | convolution fusion | flops 1647378432 | bytes 27525120 | tf_op jit(solution)/shard_map/while/body/dot_general | solution.py:37
  117.0 0.0 copy-done.1
  117.0 4.7 fusion.49
  121.7 7.3 %fusion.50 = f32[256,49,256]{2,1,0:T(8,128)} fusion(bf16[256,7,49]{2,1,0:T(8,128)(2,1)S(1)} %gather_fusion, f32[256,7,256]{2,0,1:T(8,128)S(1)} %fusion.49, f32[256,256]{1,0:T(8,128)S(1)} %convolution_multiply_fusion.2), kind=kOutput, calls=%fused_computation.10.clone.1 | convolution fusion | flops 45875200 | bytes 15117824 | tf_op jit(solution)/shard_map/while/body/bij,bic->bjc/dot_general | solution.py:48
  129.1 49.3 %scatter_fusion = f32[224,49,256]{2,1,0:T(8,128)} fusion(f32[224,49,256]{2,1,0:T(8,128)} %get-tuple-element.264, s32[256]{0:T(256)S(1)} %get-tuple-element.242, f32[256,49,256]{2,1,0:T(8,128)} %fusion.50), kind=kCustom, calls=%fused_computation.3.clone.1 | custom fusion | flops 3211264 | bytes 38536192 | tf_op jit(solution)/shard_map/while/body/scatter-add | solution.py:94
  178.3 0.0 copy-done.5
  178.3 0.0 reduce-scatter.2.cloned.1.call-update
  178.3 0.0 all-reduce.6.cloned.1.call-start
  178.4 14.6 %copy.36 = f32[1,224,49,256]{3,0,2,1:T(1,128)} copy(f32[1,224,49,256]{3,2,1,0:T(8,128)} %bitcast.56) | data formatting | bytes 22478848 | tf_op jit(solution)/shard_map/broadcast_in_dim | solution.py:102
  193.0 0.0 all-reduce.6.cloned.1.call-update
  193.0 0.0 all-reduce.4.cloned.1.call-start
  193.1 197.9 %reduce-scatter.2.cloned.1.call-done = f32[56,1792]{1,0:T(8,128)} async-done(((f32[1792,1792]{1,0:T(8,128)}), f32[56,1792]{1,0:T(8,128)}) %reduce-scatter.2.cloned.1.call-update) | async-done | bytes 401424 | tf_op jit(solution)/shard_map/reduce_scatter | solution.py:103
  390.9 0.0 all-reduce.4.cloned.1.call-update
  391.0 0.0 copy-done.6
  391.0 0.6 dynamic-slice
  392.2 140.3 %all-reduce.6.cloned.1.call-done = f32[1,224,49,256]{3,0,2,1:T(1,128)} async-done(((f32[1,224,49,256]{3,0,2,1:T(1,128)}), f32[1,224,49,256]{3,0,2,1:T(1,128)}) %all-reduce.6.cloned.1.call-update) | async-done | bytes 11239440
  532.5 2.0 constant_dynamic-slice_fusion
  534.4 73.3 %all-reduce.4.cloned.1.call-done = f32[56,1792]{1,0:T(8,128)} async-done(((f32[56,1792]{1,0:T(8,128)}), f32[56,1792]{1,0:T(8,128)}) %all-reduce.4.cloned.1.call-update) | async-done | bytes 401424 | tf_op jit(solution)/shard_map/psum | solution.py:104
  607.7 1.8 copy.64
  (8 shorter events, 0.0 us)
Async XLA Ops:
  7.2 59.9 %all-gather.2.cloned.1.call-start = ((), (), s32[]{:S(2)}) async-start(), calls=%async_computation.1 | async-start | bytes 6623232 | tf_op jit(solution)/shard_map/all_gather | solution.py:76
  7.9 383.0 %reduce-scatter.2.cloned.1.call-start = ((), (), s32[]{:S(2)}) async-start(), calls=%async_computation.2 | async-start | bytes 13246464 | tf_op jit(solution)/shard_map/reduce_scatter | solution.py:103
  72.6 5.4 copy-start
  72.6 5.4 copy-start.2
  72.6 5.4 copy-start.3
  72.6 5.4 copy-start.4
  105.1 11.9 %copy-start.1 = (bf16[256,7,256]{0,2,1:T(8,128)(2,1)S(1)}, bf16[256,7,256]{0,2,1:T(8,128)(2,1)}, u32[]{:S(2)}) copy-start(bf16[256,7,256]{0,2,1:T(8,128)(2,1)} %copy.50) | copy-start | bytes 2752516 | tf_op jit(solution)/shard_map/while
  129.0 49.3 %copy-start.5 = (f32[600,256]{1,0:T(8,128)S(1)}, f32[600,256]{1,0:T(8,128)}, u32[]{:S(2)}) copy-start(f32[600,256]{1,0:T(8,128)} %get-tuple-element.334) | copy-start | bytes 1843204 | tf_op jit(solution)/shard_map/while
  178.3 354.2 %all-reduce.6.cloned.1.call-start = ((), (), s32[]{:S(2)}) async-start(), calls=%async_computation.4 | async-start | bytes 22478848
  193.0 198.0 %copy-start.6 = (u32[256]{0:T(256)S(1)}, u32[256]{0:T(256)}, u32[]{:S(2)}) copy-start(u32[256]{0:T(256)} %constant.58) | copy-start | bytes 3076
  193.0 414.7 %all-reduce.4.cloned.1.call-start = ((), (), s32[]{:S(2)}) async-start(), calls=%async_computation.3 | async-start | bytes 802816 | tf_op jit(solution)/shard_map/psum | solution.py:104
Sparse Core Ops, SparseCore 0:
  10.6 56.4 all-gather.1
  178.5 212.4 reduce-scatter.1
  394.4 137.9 all-reduce.5
  534.7 72.9 all-reduce.3
where the time goes:
time: 618 us; the launch traced here: 616 us
  waiting for transfers between devices  464 us (75%)
  local copies, waits for them, and re-layouts  51.7 us (8%)
  other arithmetic  51 us (8%)
  matrix products  33.7 us (5%)
  between operations  15.1 us (2%)
    reduce_scatter x1, waiting for transfers between devices, per_device(): lax.psum_scatter(weight_acc, 'graph', scatter_dimension=0, tiled=True)  198 us
    unnamed x5, waiting for transfers between devices  141 us
    psum x1, waiting for transfers between devices, per_device(): weight_grad = lax.psum(rows_part, 'dp')  73.3 us
    all_gather x1, waiting for transfers between devices, per_device(): sources_all = lax.all_gather(node_feats, 'graph', axis=1, tiled=True)[0]  52 us
    scatter-add x1, other arithmetic, advance(): node_acc.at[here_source].add(spread_back(turning, returned))  49.3 us
    broadcast_in_dim x1, local copies, waits for them, and re-layouts, per_device(): node_acc[None]  14.6 us
  transfers between devices with their start and end apart: 4, of which 4 were waited for; matrix products, arithmetic and copies ran while one was open for 4% of the time, Pallas kernels for 0%

commit v1 on v0

--- a/solution.py
+++ b/solution.py
@@ -101,7 +101,11 @@
     weight_acc, node_acc = lax.fori_loop(0, blocks, advance, start_state)
     node_part = lax.psum_scatter(node_acc[None], "graph", scatter_dimension=1, tiled=True)
     rows_part = lax.psum_scatter(weight_acc, "graph", scatter_dimension=0, tiled=True)
-    weight_grad = lax.psum(rows_part, "dp")
+    weight_grad = rows_part
+    for hop in (1, 2, 4):
+        weight_grad = weight_grad + lax.ppermute(
+            weight_grad, "dp", [(dev, dev ^ hop) for dev in range(8)]
+        )
     return (node_part, weight_grad)
 
 

time: 618 us -> 545 us (0.88)
  waiting for transfers between devices: 464 us -> 380 us
  starting transfers between devices: 0.16 us -> 10.3 us
    psum x1 -> x0, waiting for transfers between devices: 73.3 us -> none  [per_device(): weight_grad = lax.psum(rows_part, 'dp')]
    unnamed x5 -> x4, waiting for transfers between devices: 141 us -> 106 us
    ppermute x0 -> x3, waiting for transfers between devices: none -> 24.6 us  [per_device(): lax.ppermute(weight_grad, 'dp', [(dev, dev ^ hop) for dev in range(8)])]
    ppermute x0 -> x3, starting transfers between devices: none -> 9.92 us  [per_device(): lax.ppermute(weight_grad, 'dp', [(dev, dev ^ hop) for dev in range(8)])]
  transfers between devices with their start and end apart: 4 -> 6, of which waited for: 4 -> 5; matrix products, arithmetic and copies ran while one was open for 4% -> 5% of each run, Pallas kernels for 0% -> 0%
where the time goes in v1:
time: 545 us; the launch traced here: 542 us
  waiting for transfers between devices  380 us (70%)
  other arithmetic  53 us (10%)
  local copies, waits for them, and re-layouts  49.9 us (9%)
  matrix products  33.7 us (6%)
  between operations  15.1 us (3%)
  starting transfers between devices  10.3 us (2%)
    reduce_scatter x1, waiting for transfers between devices, per_device(): lax.psum_scatter(weight_acc, 'graph', scatter_dimension=0, tiled=True)  197 us
    unnamed x4, waiting for transfers between devices  106 us
    all_gather x1, waiting for transfers between devices, per_device(): sources_all = lax.all_gather(node_feats, 'graph', axis=1, tiled=True)[0]  52 us
    scatter-add x1, other arithmetic, advance(): node_acc.at[here_source].add(spread_back(turning, returned))  49.3 us
    ppermute x3, waiting for transfers between devices, per_device(): lax.ppermute(weight_grad, 'dp', [(dev, dev ^ hop) for dev in range(8)])  24.6 us
    broadcast_in_dim x1, local copies, waits for them, and re-layouts, per_device(): node_acc[None]  14.6 us
    dot_general x1, matrix products, backward_terms(): lax.dot_general(flat_in, flat_grad, (((0,), (0,)), ((), ())), preferred_e...  11.9 us
  transfers between devices with their start and end apart: 6, of which 5 were waited for; matrix products, arithmetic and copies ran while one was open for 5% of the time, Pallas kernels for 0%

profile of v1, /device:TPU:2, one launch (start us, length us, event | category | flops | bytes accessed | tf_op | source)
XLA Modules:
  0.0 541.9 jit_solution(14273511647557770852)
XLA Ops:
  7.2 0.0 all-gather.2.cloned.1.call-start
  7.2 0.7 all-gather.2.cloned.1.call-update
  7.9 0.0 reduce-scatter.2.cloned.1.call-start
  8.6 5.6 %copy.34 = bf16[2048,7,49]{2,1,0:T(8,128)(2,1)} copy(bf16[2048,7,49]{0,2,1:T(8,128)(2,1)} %param.21) | data formatting | bytes 2809856 | tf_op jit(solution)/shard_map/while | solution.py:101
  14.2 0.9 select_reduce_fusion
  15.1 52.0 %all-gather.2.cloned.1.call-done = bf16[1,224,49,256]{3,2,0,1:T(8,128)(2,1)} async-done(((bf16[1,7,49,256]{3,2,0,1:T(8,128)(2,1)}), bf16[1,224,49,256]{3,2,0,1:T(8,128)(2,1)}) %all-gather.2.cloned.1.call-update) | async-done | bytes 5619728 | tf_op jit(solution)/shard_map/all_gather | solution.py:76
  67.1 5.5 %broadcast_in_dim.44 = f32[1792,1792]{1,0:T(8,128)} broadcast(f32[]{:T(128)} %constant.41.clone.1), dimensions={} | broadcast | bytes 12845060 | tf_op jit(solution)/shard_map/broadcast_in_dim | solution.py:98
  72.6 5.4 broadcast_in_dim.45
  78.1 0.0 copy-done
  78.1 0.0 copy-done.2
  78.1 0.0 copy-done.3
  78.1 0.0 copy-done.4
  78.1 100.3 %while.12 = (s32[]{:T(128)}, f32[1792,1792]{1,0:T(8,128)}, f32[224,49,256]{2,1,0:T(8,128)}, s32[]{:T(128)}, s32[512]{0:T(512)S(1)}, /*index=5*/bf16[2048,7,49]{2...) while((s32[]{:T(128)}, f32[1792,1792]{1,0:T(8,128)}, ...), condition=%wide.region_4.5_spmd, body=%wide.region_2.4_spmd.sunk | while | flops 3904316672 | bytes 142397968 | solution.py:101
  78.3 0.1 compare_select_fusion.5
  78.4 3.0 gather_fusion
  81.4 0.1 compare_select_fusion.6
  81.5 6.8 %gather_fusion.1 = bf16[256,49,256]{2,1,0:T(8,128)(2,1)} fusion(bf16[224,49,256]{2,1,0:T(8,128)(2,1)} %get-tuple-element.287, s32[1024]{0:T(1024)S(1)} %pad_clamp_fusion.7), kind=kCustom, calls=%fused_computation.1.clone.1 | custom fusion | bytes 12846080 | tf_op jit(solution)/shard_map/while/body/gather | solution.py:88
  88.3 0.1 dynamic_slice.20
  88.4 0.6 compare_convert_fusion.2
  89.0 0.9 convolution_multiply_fusion.2
  89.9 4.4 multiply_convert_fusion.2
  94.4 0.8 copy.49
  95.2 4.0 gather_fusion.2
  99.2 4.4 convolution_convert_fusion.2
  103.6 1.6 copy.50
  105.2 11.9 %convolution_add_fusion.2 = f32[1792,1792]{1,0:T(8,128)} fusion(f32[1792,1792]{1,0:T(8,128)} %get-tuple-element.263, bf16[256,1792]{0,1:T(8,128)(2,1)S(1)} %bitcast.58, bf16[256,1792]{0,1:T(8,128)(2,1)} %bitcast.59), kind=kOutput, calls=%fused_computation.4.clone.1 | convolution fusion | flops 1647378432 | bytes 27525120 | tf_op jit(solution)/shard_map/while/body/dot_general | solution.py:37
  117.1 0.0 copy-done.1
  117.1 4.7 fusion.49
  121.8 7.3 %fusion.50 = f32[256,49,256]{2,1,0:T(8,128)} fusion(bf16[256,7,49]{2,1,0:T(8,128)(2,1)S(1)} %gather_fusion, f32[256,7,256]{2,0,1:T(8,128)S(1)} %fusion.49, f32[256,256]{1,0:T(8,128)S(1)} %convolution_multiply_fusion.2), kind=kOutput, calls=%fused_computation.10.clone.1 | convolution fusion | flops 45875200 | bytes 15117824 | tf_op jit(solution)/shard_map/while/body/bij,bic->bjc/dot_general | solution.py:48
  129.1 49.3 %scatter_fusion = f32[224,49,256]{2,1,0:T(8,128)} fusion(f32[224,49,256]{2,1,0:T(8,128)} %get-tuple-element.264, s32[256]{0:T(256)S(1)} %get-tuple-element.242, f32[256,49,256]{2,1,0:T(8,128)} %fusion.50), kind=kCustom, calls=%fused_computation.3.clone.1 | custom fusion | flops 3211264 | bytes 38536192 | tf_op jit(solution)/shard_map/while/body/scatter-add | solution.py:94
  178.4 0.0 copy-done.5
  178.4 0.0 reduce-scatter.2.cloned.1.call-update
  178.4 0.3 all-reduce.3.cloned.1.call-start
  178.7 14.6 %copy.36 = f32[1,224,49,256]{3,0,2,1:T(1,128)} copy(f32[1,224,49,256]{3,2,1,0:T(8,128)} %bitcast.56) | data formatting | bytes 22478848 | tf_op jit(solution)/shard_map/broadcast_in_dim | solution.py:102
  193.3 0.0 all-reduce.3.cloned.1.call-update
  193.3 197.5 %reduce-scatter.2.cloned.1.call-done = f32[56,1792]{1,0:T(8,128)} async-done(((f32[1792,1792]{1,0:T(8,128)}), f32[56,1792]{1,0:T(8,128)}) %reduce-scatter.2.cloned.1.call-update) | async-done | bytes 401424 | tf_op jit(solution)/shard_map/reduce_scatter | solution.py:103
  390.8 1.5 collective-permute-start
  392.3 8.6 %collective-permute-done = f32[56,1792]{1,0:T(8,128)S(1)} collective-permute-done((f32[56,1792]{1,0:T(8,128)}, f32[56,1792]{1,0:T(8,128)S(1)}, u32[]{:S(2)}, u32[]{:S(2)}) %collective-permute-start) | collective-permute-done | bytes 401440 | tf_op jit(solution)/shard_map/ppermute | solution.py:106
  400.9 1.1 add.52
  402.0 2.6 collective-permute-start.1
  404.6 16.0 %collective-permute-done.1 = f32[56,1792]{1,0:T(8,128)S(1)} collective-permute-done((f32[56,1792]{1,0:T(8,128)S(1)}, f32[56,1792]{1,0:T(8,128)S(1)}, u32[]{:S(2)}, u32[]{:S(2)}) %collective-permute-start.1) | collective-permute-done | bytes 401440 | tf_op jit(solution)/shard_map/ppermute | solution.py:106
  420.6 0.1 add.53
  420.7 5.8 %collective-permute-start.2 = (f32[56,1792]{1,0:T(8,128)S(1)}, f32[56,1792]{1,0:T(8,128)S(1)}, u32[]{:S(2)}, u32[]{:S(2)}) collective-permute-start(f32[56,1792]{1,0:T(8,128)S(1)} %add.53), channel_id=1, source_target_pairs={{0,128},{32,160},{64,192},{96,224},{128,0},{160,32},{192,64},{224,... | collective-permute-start | bytes 1204232 | tf_op jit(solution)/shard_map/ppermute | solution.py:106
  426.5 0.6 dynamic-slice
  427.7 104.9 %all-reduce.3.cloned.1.call-done = f32[1,224,49,256]{3,0,2,1:T(1,128)} async-done(((f32[1,224,49,256]{3,0,2,1:T(1,128)}), f32[1,224,49,256]{3,0,2,1:T(1,128)}) %all-reduce.3.cloned.1.call-update) | async-done | bytes 11239440
  532.6 2.0 constant_dynamic-slice_fusion
  534.6 0.0 collective-permute-done.2
  534.6 0.8 add.54
  (13 shorter events, 0.0 us)
Async XLA Ops:
  7.2 59.9 %all-gather.2.cloned.1.call-start = ((), (), s32[]{:S(2)}) async-start(), calls=%async_computation.1 | async-start | bytes 6623232 | tf_op jit(solution)/shard_map/all_gather | solution.py:76
  7.9 382.9 %reduce-scatter.2.cloned.1.call-start = ((), (), s32[]{:S(2)}) async-start(), calls=%async_computation.2 | async-start | bytes 13246464 | tf_op jit(solution)/shard_map/reduce_scatter | solution.py:103
  72.6 5.4 %copy-start = (bf16[1,7,49,256]{3,2,1,0:T(8,128)(2,1)S(1)}, bf16[1,7,49,256]{3,2,1,0:T(8,128)(2,1)}, u32[]{:S(2)}) copy-start(bf16[1,7,49,256]{3,2,1,0:T(8,128)(2,1)} %param.14) | copy-start | bytes 526852
  72.6 5.4 %copy-start.2 = (s32[1,512]{1,0:T(1,128)S(1)}, s32[1,512]{1,0:T(1,128)}, u32[]{:S(2)}) copy-start(s32[1,512]{1,0:T(1,128)} %param.18) | copy-start | bytes 6148
  72.6 5.4 %copy-start.3 = (f32[1,512]{1,0:T(1,128)S(1)}, f32[1,512]{1,0:T(1,128)}, u32[]{:S(2)}) copy-start(f32[1,512]{1,0:T(1,128)} %param.19) | copy-start | bytes 6148
  72.6 5.4 %copy-start.4 = (f32[600,256]{1,0:T(8,128)S(1)}, f32[600,256]{1,0:T(8,128)}, u32[]{:S(2)}) copy-start(f32[600,256]{1,0:T(8,128)} %param.23) | copy-start | bytes 1843204
  105.2 11.9 %copy-start.1 = (bf16[256,7,256]{0,2,1:T(8,128)(2,1)S(1)}, bf16[256,7,256]{0,2,1:T(8,128)(2,1)}, u32[]{:S(2)}) copy-start(bf16[256,7,256]{0,2,1:T(8,128)(2,1)} %copy.50) | copy-start | bytes 2752516 | tf_op jit(solution)/shard_map/while
  129.1 49.3 %copy-start.5 = (f32[600,256]{1,0:T(8,128)S(1)}, f32[600,256]{1,0:T(8,128)}, u32[]{:S(2)}) copy-start(f32[600,256]{1,0:T(8,128)} %get-tuple-element.334) | copy-start | bytes 1843204 | tf_op jit(solution)/shard_map/while
  178.4 354.2 %all-reduce.3.cloned.1.call-start = ((), (), s32[]{:S(2)}) async-start(), calls=%async_computation.3 | async-start | bytes 22478848
  193.3 233.2 %copy-start.6 = (u32[256]{0:T(256)S(1)}, u32[256]{0:T(256)}, u32[]{:S(2)}) copy-start(u32[256]{0:T(256)} %constant.58) | copy-start | bytes 3076
  390.8 10.2 %collective-permute-start = (f32[56,1792]{1,0:T(8,128)}, f32[56,1792]{1,0:T(8,128)S(1)}, u32[]{:S(2)}, u32[]{:S(2)}) collective-permute-start(f32[56,1792]{1,0:T(8,128)} %reduce-scatter.2.cloned.1.call-done), channel_id=1, source_target_pairs={{0,32},{32,0},{64,96},{96,64},{128,160},{160,128},{192,224},{224,1... | collective-permute-start | bytes 1204232 | tf_op jit(solution)/shard_map/ppermute | solution.py:106
  402.0 18.6 %collective-permute-start.1 = (f32[56,1792]{1,0:T(8,128)S(1)}, f32[56,1792]{1,0:T(8,128)S(1)}, u32[]{:S(2)}, u32[]{:S(2)}) collective-permute-start(f32[56,1792]{1,0:T(8,128)S(1)} %add.52), channel_id=1, source_target_pairs={{0,64},{32,96},{64,0},{96,32},{128,192},{160,224},{192,128},{224,1... | collective-permute-start | bytes 1204232 | tf_op jit(solution)/shard_map/ppermute | solution.py:106
  420.7 113.9 %collective-permute-start.2 = (f32[56,1792]{1,0:T(8,128)S(1)}, f32[56,1792]{1,0:T(8,128)S(1)}, u32[]{:S(2)}, u32[]{:S(2)}) collective-permute-start(f32[56,1792]{1,0:T(8,128)S(1)} %add.53), channel_id=1, source_target_pairs={{0,128},{32,160},{64,192},{96,224},{128,0},{160,32},{192,64},{224,... | collective-permute-start | bytes 1204232 | tf_op jit(solution)/shard_map/ppermute | solution.py:106
Sparse Core Ops, SparseCore 0:
  10.6 56.4 all-gather.1
  178.6 212.1 reduce-scatter.1
  394.3 138.2 all-reduce.2
